TPU v7x, 256 devices: a whole 4x4x8 slice. The times are simulated.
256 devices in a mesh: group: 8 (over y, core), worker: 32 (over x, z).
Axes of the slice: x: 4, y: 4, z: 8, core: 2. Of those that a mesh axis runs over, the one named last changes fastest.
Arguments:
- green_tensor: bfloat16 [4096, 1024], P(('group', 'worker')), may hold values from -0.09375 to 0.09375
- slip_field: float32 [4096, 256], P(('group', 'worker')), may hold values from 0.1 to 3
- rupture_time: float32 [4096, 256], P(('group', 'worker')), may hold values from 0 to 40
- periods: float32 [256], replicated, may hold values from 1 to 10
- owner_map: int32 [256, 1], replicated, may hold values from 0 to 31; in each aligned block of 32 rows (0 to 31, 32 to 63, ...) at most 3 rows name the same one
Outputs:
- spectra_slots: float32 [768, 512], P(('group', 'worker'))
Inputs may be any that keep to these rules, and one draw needn't show every extreme that they name: `owner_map`: in each aligned block of 1 * 32 rows (one group's variations) no worker is named by more than 3 rows; in some block one worker is named by exactly 3.
All inputs are finite; a program needn't handle non-finite values.
Results may differ from a plain program's by a relative error of at most 0.0024.
Values sent between devices are 32-bit elements; how exact they have to be, the bound alone decides.
A program may use at most 64 MiB of HBM per device.

v0:
```python
import math

import jax
import jax.numpy as jnp
from jax import lax
from jax.sharding import PartitionSpec as P

NT = 4096
NF = 256
NP = 256
V_DEV = 1
MOST = 3


time_step = 0.05
damping = 0.05


def angular_grid():
    return 2.0 * math.pi * jnp.arange(NF, dtype=jnp.float32) / (NT * time_step)


def oscillator_gains(periods):
    natural = 2.0 * math.pi / periods
    angular = angular_grid()
    denom_real = natural[:, None] ** 2 - angular[None, :] ** 2
    denom_imag = 2.0 * damping * natural[:, None] * angular[None, :]
    modulus = denom_real**2 + denom_imag**2
    scale = natural[:, None] ** 2 / modulus
    return (-scale * denom_real, scale * denom_imag)


def basis_table():
    freq_index = jnp.arange(NF, dtype=jnp.int32)
    time_index = jnp.arange(NT, dtype=jnp.int32)
    turns = freq_index[:, None] * time_index[None, :] % NT
    angle_grid = 2.0 * math.pi / NT * turns.astype(jnp.float32)
    fold_weight = jnp.where(freq_index == 0, 1.0, 2.0).astype(jnp.float32)[:, None]
    return jnp.concatenate(
        [fold_weight * jnp.cos(angle_grid), -fold_weight * jnp.sin(angle_grid)], 0
    ).astype(jnp.bfloat16)


def slot_selector(owner_map, groups, workers):
    owners = owner_map[:, 0].reshape(groups, V_DEV * workers)
    matches = (owners[:, :, None] == jnp.arange(workers, dtype=jnp.int32)[None, None, :]).astype(
        jnp.int32
    )
    ranking = jnp.cumsum(matches, axis=1) - 1
    slot_index = jnp.sum(matches * ranking, axis=2)
    hits = owners[:, None, None, :] == jnp.arange(workers, dtype=jnp.int32)[None, :, None, None]
    hits = hits & (
        slot_index[:, None, None, :] == jnp.arange(MOST, dtype=jnp.int32)[None, None, :, None]
    )
    return hits.astype(jnp.float32)


def reduce_rows(buffer):
    partly = lax.psum_scatter(buffer, "worker", scatter_dimension=0, tiled=True)
    return lax.psum_scatter(partly, "group", scatter_dimension=0, tiled=True)


def peak_rows(spectra_rows, gain_real, gain_imag, basis):
    count = spectra_rows.shape[0]
    single = spectra_rows.reshape(count, 2, 2, NF)
    spec_real = single[:, :, 0][:, :, None, :]
    spec_imag = single[:, :, 1][:, :, None, :]
    weighted_real = spec_real * gain_real - spec_imag * gain_imag
    weighted_imag = spec_real * gain_imag + spec_imag * gain_real
    weighted = jnp.concatenate([weighted_real, weighted_imag], -1).astype(jnp.bfloat16)
    weighted = weighted.reshape(count * 2 * NP, 2 * NF)
    response = jnp.dot(weighted, basis, preferred_element_type=jnp.float32)
    peak_flat = jnp.max(jnp.abs(response), axis=1) / math.sqrt(NF)
    return peak_flat.reshape(count, 2 * NP)


def local(green_tensor, slip_field, rupture_time, periods, owner_map):
    groups = lax.axis_size("group")
    workers = lax.axis_size("worker")
    high = lax.Precision.HIGHEST
    local_count = green_tensor.shape[0]
    angular = angular_grid()
    green = green_tensor.reshape(local_count, 2, 2, NF)
    green_real = green[:, :, 0, :]
    green_imag = green[:, :, 1, :]
    phase = angular[None, None, :] * rupture_time[:, :, None]
    cos_part = (
        (slip_field[:, :, None] * jnp.cos(phase))
        .astype(jnp.bfloat16)
        .reshape(local_count, groups, workers, V_DEV, NF)
    )
    sin_part = (
        (slip_field[:, :, None] * jnp.sin(phase))
        .astype(jnp.bfloat16)
        .reshape(local_count, groups, workers, V_DEV, NF)
    )
    gain_real, gain_imag = oscillator_gains(periods)
    basis = basis_table()
    selector = slot_selector(owner_map, groups, workers)
    f32 = jnp.float32
    real_part = jnp.einsum(
        "sgwik,sck->gwick", cos_part, green_real, preferred_element_type=f32
    ) + jnp.einsum("sgwik,sck->gwick", sin_part, green_imag, preferred_element_type=f32)
    imag_part = jnp.einsum(
        "sgwik,sck->gwick", cos_part, green_imag, preferred_element_type=f32
    ) - jnp.einsum("sgwik,sck->gwick", sin_part, green_real, preferred_element_type=f32)
    partial_value = jnp.stack([real_part, imag_part], axis=-2).reshape(
        groups, V_DEV * workers, 4 * NF
    )
    buffer = jnp.einsum("gojv,gvx->ogjx", selector, partial_value, precision=high)
    summed = reduce_rows(buffer.reshape(-1, 4 * NF))
    return peak_rows(summed, gain_real, gain_imag, basis)


def solution(mesh):
    placed = (
        P(("group", "worker"), None),
        P(("group", "worker"), None),
        P(("group", "worker"), None),
        P(),
        P(),
    )
    return jax.shard_map(
        local, mesh=mesh, in_specs=placed, out_specs=P(("group", "worker"), None), check_vma=False
    )
```

profile of v0, /device:TPU:1, one launch (start us, length us, event | category | flops | bytes accessed | tf_op | source)
XLA Modules:
  0.0 566.5 jit_solution(11337169579034334873)
XLA Ops:
  6.5 0.0 reduce-scatter.2.cloned.1.call-start
  6.5 0.5 broadcast.200
  7.1 1.3 reduce.3
  8.4 0.1 eq.68
  8.5 0.1 copy.31
  8.6 0.8 mul.188
  9.4 0.8 mul.191
  10.2 0.8 reshape.218
  11.0 0.1 fusion.57
  11.1 0.1 copy.40
  11.2 0.1 copy.39
  11.4 57.7 %fusion.6 = f32[256,8,32,2]{2,3,1,0:T(2,128)S(1)} fusion(f32[16,8,32]{2,0,1:T(8,128)S(1)} %copy.27, f32[256]{0:T(256)S(1)} %get-tuple-element.15, f32[16,8,32]{2,0,1:T(8,128)S(1)} %copy.26, bf16[16,2,1,256]{0,1,3,2:T(2,128)(2,1)S(1)} %copy.40), kind=kOutput, calls=%fused_computation.8 | convolution fusion | flops 7340032 | bytes 574464 | tf_op jit(solution)/shard_map/sgwik,sck->gwick/dot_general | solution.py:103
  69.0 57.6 %fusion.4 = f32[256,8,32,2]{2,3,1,0:T(2,128)S(1)} fusion(f32[16,8,32]{2,0,1:T(8,128)S(1)} %copy.27, f32[256]{0:T(256)S(1)} %get-tuple-element.15, f32[16,8,32]{2,0,1:T(8,128)S(1)} %copy.26, bf16[16,2,1,256]{0,1,3,2:T(2,128)(2,1)S(1)} %copy.39), kind=kOutput, calls=%fused_computation.7 | convolution fusion | flops 7340032 | bytes 574464 | tf_op jit(solution)/shard_map/sgwik,sck->gwick/dot_general | solution.py:106
  126.7 57.5 %add_bitcast_fusion = f32[8,32,1,2,1,256]{1,3,0,5,4,2:T(2,128)S(1)} fusion(f32[256,8,32,2]{2,3,1,0:T(2,128)S(1)} %fusion.6, f32[16,8,32]{2,0,1:T(8,128)S(1)} %copy.27, f32[256]{0:T(256)S(1)} %get-tuple-element.15, f32[16,8,32]{2,0,1:T(8,128)S(1)} %copy.26, bf16[16,2,1,256]{0,1,3,2:T(2,128)(2,1)S(1)} %copy.39), kind=kOutput, calls=%fused_computation.39 | convolution fusion | flops 7471104 | bytes 1098752 | tf_op jit(solution)/shard_map/sgwik,sck->gwick/dot_general | solution.py:101
  184.2 57.7 %subtract_bitcast_fusion = f32[8,32,1,2,1,256]{1,3,0,5,4,2:T(2,128)S(1)} fusion(f32[256,8,32,2]{2,3,1,0:T(2,128)S(1)} %fusion.4, f32[16,8,32]{2,0,1:T(8,128)S(1)} %copy.27, f32[256]{0:T(256)S(1)} %get-tuple-element.15, f32[16,8,32]{2,0,1:T(8,128)S(1)} %copy.26, bf16[16,2,1,256]{0,1,3,2:T(2,128)(2,1)S(1)} %copy.40), kind=kOutput, calls=%fused_computation.38 | convolution fusion | flops 7471104 | bytes 1098752 | tf_op jit(solution)/shard_map/sgwik,sck->gwick/dot_general | solution.py:104
  241.9 4.1 pad_maximum_fusion
  246.0 5.3 copy.30
  251.3 0.8 reshape.224
  252.1 0.7 fusion.59
  252.8 0.1 copy.32
  252.9 1.4 convolution_bitcast_fusion
  254.3 4.1 copy.33
  258.4 0.0 copy-start
  258.4 6.0 %reshape.220 = f32[768,1024]{1,0:T(8,128)} reshape(f32[32,8,3,1024]{3,2,1,0:T(4,128)} %copy.33) | data formatting | bytes 6291456 | tf_op jit(solution)/shard_map/reshape | solution.py:111
  264.4 0.0 copy-start.1
  264.4 0.0 reduce-scatter.2.cloned.1.call-update
  264.4 0.0 all-reduce.3.cloned.1.call-start
  264.4 0.0 copy-done
  264.5 18.1 %multiply_convert_fusion = (bf16[256,4096]{1,0:T(8,128)(2,1)S(1)}, bf16[256,4096]{1,0:T(8,128)(2,1)}) fusion(f32[256]{0:T(256)S(1)} %fusion.54, f32[256]{0:T(256)S(1)} %compare_select_fusion), kind=kLoop, calls=%fused_computation.33 | loop fusion | flops 18874368 | bytes 4196352 | tf_op jit(solution)/shard_map/convert.1
  282.6 200.0 %reduce-scatter.2.cloned.1.call-done = f32[24,1024]{1,0:T(8,128)} async-done(((f32[768,1024]{1,0:T(8,128)}), f32[24,1024]{1,0:T(8,128)}) %reduce-scatter.2.cloned.1.call-update) | async-done | bytes 98320 | tf_op jit(solution)/shard_map/reduce_scatter | solution.py:59
  482.6 0.0 all-reduce.3.cloned.1.call-update
  482.6 0.2 subtract_multiply_fusion
  482.8 0.0 copy-done.1
  482.8 0.6 dynamic-slice
  484.0 64.9 %all-reduce.3.cloned.1.call-done = f32[24,1024]{1,0:T(8,128)} async-done(((f32[24,1024]{1,0:T(8,128)}), f32[24,1024]{1,0:T(8,128)}) %all-reduce.3.cloned.1.call-update) | async-done | bytes 98320
  548.9 0.8 constant_dynamic-slice_fusion
  549.9 0.4 subtract_convert_fusion
  550.3 8.7 %abs_reduce_fusion = f32[1536]{0:T(1024)S(1)} fusion(bf16[256,4096]{1,0:T(8,128)(2,1)S(1)} %get-tuple-element.17, bf16[256,4096]{1,0:T(8,128)(2,1)} %get-tuple-element.18, bf16[1536,256]{1,0:T(8,128)(2,1)S(1)} %bitcast.55, bf16[1536,256]{1,0:T(8,128)(2,1)S(1)} %bitcast.54), kind=kOutput, calls=%fused_computation | convolution fusion | flops 6466566656 | bytes 5773312 | tf_op jit(solution)/shard_map/dot_general | solution.py:72
  559.0 0.6 div.43
  (13 shorter events, 0.1 us)
Async XLA Ops:
  6.5 476.1 %reduce-scatter.2.cloned.1.call-start = ((), (), s32[]{:S(2)}) async-start(), calls=%async_computation.1 | async-start | bytes 3244032 | tf_op jit(solution)/shard_map/reduce_scatter | solution.py:59
  258.4 6.1 %copy-start = (f32[256]{0:T(256)S(1)}, f32[256]{0:T(256)}, u32[]{:S(2)}) copy-start(f32[256]{0:T(256)} %param.8) | copy-start | bytes 3076
  264.4 218.4 %copy-start.1 = (u32[256]{0:T(256)S(1)}, u32[256]{0:T(256)}, u32[]{:S(2)}) copy-start(u32[256]{0:T(256)} %constant.48) | copy-start | bytes 3076
  264.4 284.6 %all-reduce.3.cloned.1.call-start = ((), (), s32[]{:S(2)}) async-start(), calls=%async_computation.2 | async-start | bytes 196608
Sparse Core Ops, SparseCore 0:
  264.5 218.0 reduce-scatter.1
  485.0 63.8 all-reduce.2
where the time goes:
time: 568 us; the launch traced here: 566 us
  waiting for transfers between devices  265 us (47%)
  matrix products  241 us (42%)
  other arithmetic  24.9 us (4%)
  local copies, waits for them, and re-layouts  21.7 us (4%)
  between operations  14.2 us (2%)
    reduce_scatter x1, waiting for transfers between devices, reduce_rows(): partly = lax.psum_scatter(buffer, 'worker', scatter_dimension=0, tiled=True)  200 us
    unnamed x3, waiting for transfers between devices  64.9 us
    dot_general x1, matrix products, local(): jnp.einsum('sgwik,sck->gwick', cos_part, green_imag, preferred_element_ty...  57.7 us
    dot_general x1, matrix products, local(): jnp.einsum('sgwik,sck->gwick', sin_part, green_imag, preferred_element_ty...  57.7 us
    dot_general x1, matrix products, local(): jnp.einsum('sgwik,sck->gwick', sin_part, green_real, preferred_element_ty...  57.6 us
    dot_general x1, matrix products, local(): jnp.einsum('sgwik,sck->gwick', cos_part, green_real, preferred_element_ty...  57.5 us
    another operation x2, other arithmetic  18.5 us
  transfers between devices with their start and end apart: 2, of which 2 were waited for; matrix products, arithmetic and copies ran while one was open for 3% of the time, Pallas kernels for 0%

commit v1 on v0

v1 whole, which is shorter than its diff:
```python
import functools
import math

import jax
import jax.numpy as jnp
from jax import lax
from jax.experimental import pallas as pl
from jax.experimental.pallas import tpu as pltpu
from jax.sharding import PartitionSpec as P

NT = 4096
NF = 256
NP = 256
MOST = 3
TIME_STEP = 0.05
DAMPING = 0.05

GROUPS = 8
WORKERS = 32
ROWS = 16
GATHERED = ROWS * GROUPS
HALF = 128
STEPS = 64
TIMES = NT // 2 + 16

f32 = jnp.float32
bf16 = jnp.bfloat16
MESH = pl.DeviceIdType.MESH


def cos_sin_turns(turns):
    near = turns - jnp.round(turns)
    angle = near * (2.0 * math.pi)
    square = angle * angle
    cos = f32(0.0)
    for n in range(8, -1, -1):
        cos = cos * square + f32((-1) ** n / math.factorial(2 * n))
    sin = f32(0.0)
    for n in range(8, -1, -1):
        sin = sin * square + f32((-1) ** n / math.factorial(2 * n + 1))
    return cos, sin * angle


def kernel(
    green_ref, slip_ref, time_ref, periods_ref, owner_ref, out_ref,
    basis, green_stage, field_stage, green_all, field_all, phasors, lhs, spectra,
    partial, arrived, halves, peaks, gain, chosen,
    field_send, field_recv, green_send, green_recv,
    sum_send, sum_recv, half_send, half_recv, peak_send, peak_recv,
):
    group = lax.axis_index("group")
    worker = lax.axis_index("worker")
    row, core = group // 2, group % 2

    barrier = pltpu.get_barrier_semaphore()
    for i in range(1, GROUPS):
        pl.semaphore_signal(
            barrier, inc=1, device_id={"group": (group + i) % GROUPS}, device_id_type=MESH
        )
    for i in range(1, WORKERS):
        pl.semaphore_signal(
            barrier, inc=1, device_id={"worker": (worker + i) % WORKERS}, device_id_type=MESH
        )

    with jax.named_scope("stage"):
        for y in range(GROUPS // 2):
            lanes = slice(64 * y, 64 * y + 64)
            field_stage[y] = jnp.concatenate([slip_ref[:, lanes], time_ref[:, lanes]], axis=1)
        for c in range(2):
            for part in range(4):
                start = part * NF + c * HALF
                green_stage[c, :, part * HALF : (part + 1) * HALF] = green_ref[
                    :, start : start + HALF
                ].astype(f32)

    with jax.named_scope("barrier"):
        pl.semaphore_wait(barrier, GROUPS - 1 + WORKERS - 1)

    mine = pl.ds(pl.multiple_of(ROWS * group, ROWS), ROWS)
    sent = []
    with jax.named_scope("send_fields"):
        for i in range(1, GROUPS):
            to = (group + i) % GROUPS
            copy = pltpu.make_async_remote_copy(
                src_ref=field_stage.at[to // 2],
                dst_ref=field_all.at[mine],
                send_sem=field_send,
                recv_sem=field_recv,
                device_id={"group": to},
                device_id_type=MESH,
            )
            copy.start()
        for i in range(1, GROUPS):
            to = (group + i) % GROUPS
            copy = pltpu.make_async_remote_copy(
                src_ref=green_stage.at[to % 2],
                dst_ref=green_all.at[mine],
                send_sem=green_send,
                recv_sem=green_recv,
                device_id={"group": to},
                device_id_type=MESH,
            )
            copy.start()
    field_all[mine, :] = field_stage[row]
    green_all[mine, :] = green_stage[core]

    with jax.named_scope("gain"):
        natural = (2.0 * math.pi) / periods_ref[...]
        column = jnp.concatenate(
            [
                jnp.transpose(jnp.broadcast_to(natural[:, :128], (128, 128))),
                jnp.transpose(jnp.broadcast_to(natural[:, 128:], (128, 128))),
            ],
            axis=0,
        )
        for h in range(2):
            index = lax.broadcasted_iota(jnp.int32, (NP, 128), 1) + 128 * h
            angular = (2.0 * math.pi) * index.astype(f32) / (NT * TIME_STEP)
            denom_real = column * column - angular * angular
            denom_imag = (2.0 * DAMPING) * column * angular
            scale = column * column / (denom_real * denom_real + denom_imag * denom_imag)
            gain[0, :, 128 * h : 128 * h + 128] = -scale * denom_real
            gain[1, :, 128 * h : 128 * h + 128] = scale * denom_imag

    with jax.named_scope("basis"):
        freq = lax.broadcasted_iota(jnp.int32, (16, NF), 1)
        time = lax.broadcasted_iota(jnp.int32, (16, NF), 0)
        fold = jnp.where(freq == 0, 1.0, 2.0)
        cos0, sin0 = cos_sin_turns((freq * time).astype(f32) * (1.0 / NT))
        cos16, sin16 = cos_sin_turns(freq.astype(f32) * (16.0 / NT))

        def advance(b, carry):
            cos, sin = carry
            rows = pl.ds(pl.multiple_of(16 * b, 16), 16)
            basis[0, rows, :] = cos.astype(bf16)
            basis[1, rows, :] = sin.astype(bf16)
            return cos * cos16 + sin * sin16, sin * cos16 - cos * sin16

        lax.fori_loop(0, TIMES // 16, advance, (fold * cos0, -fold * sin0), unroll=3)

    with jax.named_scope("owners"):
        count = jnp.int32(0)
        for i in range(WORKERS):
            hit = (owner_ref[WORKERS * group + i] == worker).astype(jnp.int32)
            for j in range(MOST):
                value = (hit * (count == j).astype(jnp.int32)).astype(f32)
                chosen[j, i] = jnp.full((4, 128), value, f32)
            count = count + hit

    with jax.named_scope("wait_fields"):
        others = pl.ds(0, ROWS * (GROUPS - 1))
        pltpu.make_async_copy(field_all.at[others], field_all.at[others], field_recv).wait()

    with jax.named_scope("phasors"):
        for s in range(0, GATHERED, 32):
            field = field_all[s : s + 32, :]
            swapped = pltpu.roll(field, 64, 1)
            lane = lax.broadcasted_iota(jnp.int32, (32, 128), 1)
            low = lane < 64
            slip = jnp.where(low, field, swapped)
            turn = jnp.where(low, swapped, field) * (1.0 / (NT * TIME_STEP))
            first = (core * HALF + jnp.where(low, 0, STEPS)).astype(f32)
            cos0, sin0 = cos_sin_turns(turn * first)
            cos1, sin1 = cos_sin_turns(turn)

            def step(k, carry, s=s, cos1=cos1, sin1=sin1):
                cos, sin = carry
                phasors[k, s : s + 32, :] = cos.astype(bf16)
                phasors[k, GATHERED + s : GATHERED + s + 32, :] = sin.astype(bf16)
                return cos * cos1 - sin * sin1, sin * cos1 + cos * sin1

            lax.fori_loop(0, STEPS, step, (slip * cos0, slip * sin0), unroll=8)

    with jax.named_scope("wait_green"):
        pltpu.make_async_copy(green_all.at[others], green_all.at[others], green_recv).wait()

    with jax.named_scope("green"):
        for c in range(2):
            for part in range(2):
                at = (2 * c + part) * HALF
                turned = jnp.transpose(green_all[:, at : at + HALF])
                for h in range(2):
                    value = turned[STEPS * h : STEPS * h + STEPS, :]
                    real = pl.ds(4 * h + 2 * c, STEPS, stride=8)
                    imag = pl.ds(4 * h + 2 * c + 1, STEPS, stride=8)
                    if part == 0:
                        lhs[0, real, :] = value
                        lhs[1, imag, :] = -value
                    else:
                        lhs[1, real, :] = value
                        lhs[0, imag, :] = value

    with jax.named_scope("spectra"):

        def product(k, _):
            rows = pl.ds(pl.multiple_of(8 * k, 8), 8)
            spectra[rows, :] = jnp.dot(
                jnp.concatenate([lhs[0, rows, :], lhs[1, rows, :]], axis=1).astype(bf16),
                phasors[k],
                preferred_element_type=f32,
            )
            return 0

        lax.fori_loop(0, STEPS, product, 0, unroll=8)

    with jax.named_scope("turn"):
        low = lax.broadcasted_iota(jnp.int32, (64, 128), 1) < 64
        for r in range(4):
            both = jnp.concatenate(
                [spectra[pl.ds(r, STEPS, stride=8), :], spectra[pl.ds(4 + r, STEPS, stride=8), :]],
                axis=0,
            )
            turned = jnp.transpose(both)
            value = jnp.where(low, turned[:64], turned[64:])
            for c in range(2):
                partial[pl.ds(4 * c + r, WORKERS, stride=8), :] = value[
                    WORKERS * c : WORKERS * c + WORKERS
                ]

    with jax.named_scope("send_sums"):
        for i in range(1, WORKERS):
            to = (worker + i) % WORKERS
            copy = pltpu.make_async_remote_copy(
                src_ref=partial.at[pl.ds(pl.multiple_of(8 * to, 8), 8)],
                dst_ref=arrived.at[worker],
                send_sem=sum_send,
                recv_sem=sum_recv,
                device_id={"worker": to},
                device_id_type=MESH,
            )
            copy.start()
        arrived[worker] = partial[pl.ds(pl.multiple_of(8 * worker, 8), 8), :]
    with jax.named_scope("wait_sums"):
        most = pl.ds(0, WORKERS - 1)
        pltpu.make_async_copy(arrived.at[most], arrived.at[most], sum_recv).wait()

    with jax.named_scope("half"):
        total = arrived[0]
        for i in range(1, WORKERS):
            total = total + arrived[i]
        halves[core] = total
        copy = pltpu.make_async_remote_copy(
            src_ref=halves.at[core],
            dst_ref=halves.at[core],
            send_sem=half_send,
            recv_sem=half_recv,
            device_id={"group": row * 2 + (1 - core)},
            device_id_type=MESH,
        )
        copy.start()
        copy.wait()

    with jax.named_scope("weigh"):
        real, imag = [], []
        for c in range(2):
            for h in range(2):
                spec_real = halves[h, pl.ds(4 * core + 2 * c, 1), :]
                spec_imag = halves[h, pl.ds(4 * core + 2 * c + 1, 1), :]
                gain_real = gain[0, :, 128 * h : 128 * h + 128]
                gain_imag = gain[1, :, 128 * h : 128 * h + 128]
                real.append((spec_real * gain_real - spec_imag * gain_imag).astype(bf16))
                imag.append((spec_real * gain_imag + spec_imag * gain_real).astype(bf16))
        weighted = [
            jnp.concatenate(
                [
                    jnp.concatenate([x[0], x[1]], axis=1),
                    jnp.concatenate([x[2], x[3]], axis=1),
                ],
                axis=0,
            )
            for x in (real, imag)
        ]

    with jax.named_scope("response"):
        contract = (((1,), (1,)), ((), ()))
        best = jnp.zeros((8, 2 * NP), f32)
        for start, size in [(256 * b, 256) for b in range(NT // 512)] + [(NT // 2, 16)]:
            even = lax.dot_general(
                basis[0, start : start + size, :], weighted[0], contract, preferred_element_type=f32
            )
            odd = lax.dot_general(
                basis[1, start : start + size, :], weighted[1], contract, preferred_element_type=f32
            )
            value = jnp.abs(even) + jnp.abs(odd)
            for t in range(0, size, 8):
                best = jnp.maximum(best, value[t : t + 8])
        top = jnp.max(best, axis=0, keepdims=True) * (1.0 / math.sqrt(NF))
        for r in range(4):
            peaks[worker, r : r + 1, :] = top[:, 128 * r : 128 * r + 128]

    with jax.named_scope("send_peaks"):
        for i in range(1, WORKERS):
            copy = pltpu.make_async_remote_copy(
                src_ref=peaks.at[worker],
                dst_ref=peaks.at[worker],
                send_sem=peak_send,
                recv_sem=peak_recv,
                device_id={"worker": (worker + i) % WORKERS},
                device_id_type=MESH,
            )
            copy.start()
    with jax.named_scope("wait_peaks"):
        pltpu.make_async_copy(peaks.at[most], peaks.at[most], peak_recv).wait()

    with jax.named_scope("place"):
        for j in range(MOST):
            total = chosen[j, 0] * peaks[0]
            for i in range(1, WORKERS):
                total = total + chosen[j, i] * peaks[i]
            for r in range(4):
                out_ref[j : j + 1, 128 * r : 128 * r + 128] = total[r : r + 1, :]

    with jax.named_scope("wait_sent"):
        pltpu.make_async_copy(field_all.at[others], field_all.at[others], field_send).wait()
        pltpu.make_async_copy(green_all.at[others], green_all.at[others], green_send).wait()
        pltpu.make_async_copy(arrived.at[most], arrived.at[most], sum_send).wait()
        pltpu.make_async_copy(peaks.at[most], peaks.at[most], peak_send).wait()


def local(green_tensor, slip_field, rupture_time, periods, owner_map):
    vmem = pl.BlockSpec(memory_space=pltpu.VMEM)
    dma = pltpu.SemaphoreType.DMA
    return pl.pallas_call(
        kernel,
        out_shape=jax.ShapeDtypeStruct((MOST, 2 * NP), f32),
        in_specs=[
            vmem,
            vmem,
            vmem,
            vmem,
            pl.BlockSpec(memory_space=pltpu.SMEM),
        ],
        out_specs=vmem,
        scratch_shapes=[
            pltpu.VMEM((2, TIMES, NF), bf16),
            pltpu.VMEM((2, ROWS, 4 * HALF), f32),
            pltpu.VMEM((GROUPS // 2, ROWS, 128), f32),
            pltpu.VMEM((GATHERED, 4 * HALF), f32),
            pltpu.VMEM((GATHERED, 128), f32),
            pltpu.VMEM((STEPS, 2 * GATHERED, 128), bf16),
            pltpu.VMEM((2, 8 * STEPS, GATHERED), f32),
            pltpu.VMEM((8 * STEPS, 128), f32),
            pltpu.VMEM((8 * WORKERS, 128), f32),
            pltpu.VMEM((WORKERS, 8, 128), f32),
            pltpu.VMEM((2, 8, 128), f32),
            pltpu.VMEM((WORKERS, 4, 128), f32),
            pltpu.VMEM((2, NP, NF), f32),
            pltpu.VMEM((MOST, WORKERS, 4, 128), f32),
        ]
        + [dma] * 10,
        compiler_params=pltpu.CompilerParams(
            collective_id=0, has_side_effects=True, vmem_limit_bytes=32 * 1024 * 1024
        ),
        name="seismogram",
    )(
        green_tensor,
        slip_field,
        rupture_time,
        periods.reshape(1, NP),
        owner_map.reshape(-1),
    )


def solution(mesh):
    placed = (
        P(("group", "worker"), None),
        P(("group", "worker"), None),
        P(("group", "worker"), None),
        P(),
        P(),
    )
    return jax.shard_map(
        local, mesh=mesh, in_specs=placed, out_specs=P(("group", "worker"), None), check_vma=False
    )
```

time: 568 us -> 39.1 us (0.07)
  waiting for transfers between devices: 265 us -> 0 us
  matrix products: 241 us -> 0 us
  Pallas kernels: 0 us -> 35.4 us
  other arithmetic: 24.9 us -> 0 us
  local copies, waits for them, and re-layouts: 21.7 us -> 3.49 us
  between operations: 14.2 us -> 0.01 us
    dot_general x6 -> x0, matrix products: 241 us -> none  [the longest x1 57.7 us: local(): jnp.einsum('sgwik,sck->gwick', cos_part, green_imag, preferred_element_ty...]
    reduce_scatter x1 -> x0, waiting for transfers between devices: 200 us -> none  [reduce_rows(): partly = lax.psum_scatter(buffer, 'worker', scatter_dimension=0, tiled=True)]
    unnamed x3 -> x0, waiting for transfers between devices: 64.9 us -> none
    pallas_call x0 -> x1, Pallas kernels: none -> 35.4 us  [local(): pl.pallas_call(kernel, out_shape=jax.ShapeDtypeStruct((MOST, 2 * NP), f32...]
    another operation x4 -> x0, other arithmetic: 23.3 us -> none
    reshape x4 -> x0, local copies, waits for them, and re-layouts: 7.62 us -> none  [the longest x1 5.97 us: local(): summed = reduce_rows(buffer.reshape(-1, 4 * NF))]
  transfers between devices with their start and end apart: 2 -> 0, of which waited for: 2 -> 0; matrix products, arithmetic and copies ran while one was open for 3% -> 0% of each run, Pallas kernels for 0% -> 0%
where the time goes in v1:
time: 39.1 us; the launch traced here: 38.9 us
  Pallas kernels  35.4 us (91%)
  local copies, waits for them, and re-layouts  3.49 us (9%)
    pallas_call x1, Pallas kernels, local(): pl.pallas_call(kernel, out_shape=jax.ShapeDtypeStruct((MOST, 2 * NP), f32...  35.4 us
    unnamed x11, local copies, waits for them, and re-layouts  3.49 us

profile of v1, /device:TPU:1, one launch (start us, length us, event | category | flops | bytes accessed | tf_op | source)
XLA Modules:
  0.0 38.9 jit_solution(15854207717106816613)
XLA Ops:
  0.0 0.0 copy-start.4
  0.0 0.0 copy-start.3
  0.0 0.7 %copy-done.4 = s32[256,1]{0,1:T(1,128)S(1)} copy-done((s32[256,1]{0,1:T(1,128)S(1)}, s32[256,1]{0,1:T(1,128)}, u32[]{:S(2)}) %copy-start.4) | copy-done | bytes 1048
  0.7 0.0 copy-done.3
  0.7 0.0 copy-start
  0.7 0.8 %copy-done = bf16[16,1024]{1,0:T(8,128)(2,1)S(1)} copy-done((bf16[16,1024]{1,0:T(8,128)(2,1)S(1)}, bf16[16,1024]{1,0:T(8,128)(2,1)}, u32[]{:S(2)}) %copy-start) | copy-done | bytes 32792
  1.5 0.0 copy-start.1
  1.5 0.7 %copy-done.1 = f32[16,256]{1,0:T(8,128)S(1)} copy-done((f32[16,256]{1,0:T(8,128)S(1)}, f32[16,256]{1,0:T(8,128)}, u32[]{:S(2)}) %copy-start.1) | copy-done | bytes 16408
  2.2 0.0 copy-start.2
  2.2 0.7 %copy-done.2 = f32[16,256]{1,0:T(8,128)S(1)} copy-done((f32[16,256]{1,0:T(8,128)S(1)}, f32[16,256]{1,0:T(8,128)}, u32[]{:S(2)}) %copy-start.2) | copy-done | bytes 16408
  2.9 35.4 %seismogram.1 = f32[3,512]{1,0:T(4,128)S(1)} custom-call(bf16[16,1024]{1,0:T(8,128)(2,1)S(1)} %copy-done, f32[16,256]{1,0:T(8,128)S(1)} %copy-done.1, f32[16,256]{1,0:T(8,128)S(1)} %copy-done.2, f32[1,256]{1,0:T(1,128)S(1)} %bitcast.2, s32[256]{0:T(256)S(1)} %bitcast.3), custom_call_target="tpu_custom_call" | custom-call | tf_op jit(solution)/shard_map/seismogram/pallas_call | solution.py:323
  38.3 0.6 %copy.7 = f32[3,512]{1,0:T(4,128)} copy(f32[3,512]{1,0:T(4,128)S(1)} %seismogram.1) | data formatting | bytes 12288
Async XLA Ops:
  0.0 0.7 %copy-start.4 = (s32[256,1]{0,1:T(1,128)S(1)}, s32[256,1]{0,1:T(1,128)}, u32[]{:S(2)}) copy-start(s32[256,1]{0,1:T(1,128)} %param.9) | copy-start | bytes 3076
  0.0 0.7 %copy-start.3 = (f32[256]{0:T(256)S(1)}, f32[256]{0:T(256)}, u32[]{:S(2)}) copy-start(f32[256]{0:T(256)} %param.8) | copy-start | bytes 3076
  0.7 0.8 %copy-start = (bf16[16,1024]{1,0:T(8,128)(2,1)S(1)}, bf16[16,1024]{1,0:T(8,128)(2,1)}, u32[]{:S(2)}) copy-start(bf16[16,1024]{1,0:T(8,128)(2,1)} %green_ref.1) | copy-start | bytes 98308
  1.5 0.7 %copy-start.1 = (f32[16,256]{1,0:T(8,128)S(1)}, f32[16,256]{1,0:T(8,128)}, u32[]{:S(2)}) copy-start(f32[16,256]{1,0:T(8,128)} %slip_ref.1) | copy-start | bytes 49156
  2.2 0.7 %copy-start.2 = (f32[16,256]{1,0:T(8,128)S(1)}, f32[16,256]{1,0:T(8,128)}, u32[]{:S(2)}) copy-start(f32[16,256]{1,0:T(8,128)} %time_ref.1) | copy-start | bytes 49156

commit v2 on v1

--- a/solution.py
+++ b/solution.py
@@ -17,7 +17,12 @@
 
 GROUPS = 8
 WORKERS = 32
+LINE = 8
 ROWS = 16
+STEPS_TO = sorted(
+    [(i // LINE, i % LINE) for i in range(1, WORKERS)],
+    key=lambda step: -min(step[0], 4 - step[0]) - min(step[1], LINE - step[1]),
+)
 GATHERED = ROWS * GROUPS
 HALF = 128
 STEPS = 64
@@ -42,26 +47,47 @@
 
 
 def kernel(
-    green_ref, slip_ref, time_ref, periods_ref, owner_ref, out_ref,
-    basis, green_stage, field_stage, green_all, field_all, phasors, lhs, spectra,
+    green_hbm, slip_hbm, time_hbm, periods_hbm, owner_hbm, out_ref,
+    green_ref, slip_ref, time_ref, periods_ref, owner_ref, basis, green_stage, field_stage, green_all, field_all, phasors, lhs, spectra,
     partial, arrived, halves, peaks, gain, chosen,
-    field_send, field_recv, green_send, green_recv,
+    load_sem, field_send, field_recv, green_send, green_recv,
     sum_send, sum_recv, half_send, half_recv, peak_send, peak_recv,
+    near, line, everyone,
 ):
     group = lax.axis_index("group")
     worker = lax.axis_index("worker")
     row, core = group // 2, group % 2
+
+    x, z = worker // LINE, worker % LINE
+
+    def tell(semaphore, dx, dz):
+        to = (x + dx) % (WORKERS // LINE) * LINE + (z + dz) % LINE
+        pl.semaphore_signal(semaphore, inc=1, device_id={"worker": to}, device_id_type=MESH)
 
     barrier = pltpu.get_barrier_semaphore()
     for i in range(1, GROUPS):
         pl.semaphore_signal(
             barrier, inc=1, device_id={"group": (group + i) % GROUPS}, device_id_type=MESH
         )
-    for i in range(1, WORKERS):
-        pl.semaphore_signal(
-            barrier, inc=1, device_id={"worker": (worker + i) % WORKERS}, device_id_type=MESH
+    loads = [
+        pltpu.make_async_copy(source, target, load_sem.at[i])
+        for i, (source, target) in enumerate(
+            [
+                (slip_hbm, slip_ref),
+                (time_hbm, time_ref),
+                (green_hbm, green_ref),
+                (periods_hbm, periods_ref),
+                (owner_hbm, owner_ref),
+            ]
         )
-
+    ]
+    for load in loads:
+        load.start()
+    for dx, dz in ((0, 1), (0, -1), (1, 0), (-1, 0)):
+        tell(barrier, dx, dz)
+
+    for load in loads[:3]:
+        load.wait()
     with jax.named_scope("stage"):
         for y in range(GROUPS // 2):
             lanes = slice(64 * y, 64 * y + 64)
@@ -74,10 +100,10 @@
                 ].astype(f32)
 
     with jax.named_scope("barrier"):
-        pl.semaphore_wait(barrier, GROUPS - 1 + WORKERS - 1)
-
+        pl.semaphore_wait(barrier, GROUPS - 1 + 4)
+
+    others, most = pl.ds(0, ROWS * (GROUPS - 1)), pl.ds(0, WORKERS - 1)
     mine = pl.ds(pl.multiple_of(ROWS * group, ROWS), ROWS)
-    sent = []
     with jax.named_scope("send_fields"):
         for i in range(1, GROUPS):
             to = (group + i) % GROUPS
@@ -90,6 +116,8 @@
                 device_id_type=MESH,
             )
             copy.start()
+        for dx, dz in ((0, 1), (0, -1), (1, 0), (-1, 0)):
+            tell(near, dx, dz)
         for i in range(1, GROUPS):
             to = (group + i) % GROUPS
             copy = pltpu.make_async_remote_copy(
@@ -104,6 +132,8 @@
     field_all[mine, :] = field_stage[row]
     green_all[mine, :] = green_stage[core]
 
+    for load in loads[3:]:
+        load.wait()
     with jax.named_scope("gain"):
         natural = (2.0 * math.pi) / periods_ref[...]
         column = jnp.concatenate(
@@ -147,8 +177,12 @@
                 chosen[j, i] = jnp.full((4, 128), value, f32)
             count = count + hit
 
+    with jax.named_scope("along_z"):
+        pl.semaphore_wait(near, 4)
+        for dz in (2, -2):
+            tell(line, 0, dz)
+
     with jax.named_scope("wait_fields"):
-        others = pl.ds(0, ROWS * (GROUPS - 1))
         pltpu.make_async_copy(field_all.at[others], field_all.at[others], field_recv).wait()
 
     with jax.named_scope("phasors"):
@@ -170,6 +204,11 @@
                 return cos * cos1 - sin * sin1, sin * cos1 + cos * sin1
 
             lax.fori_loop(0, STEPS, step, (slip * cos0, slip * sin0), unroll=8)
+
+    with jax.named_scope("along_x"):
+        pl.semaphore_wait(line, 2)
+        for dx in (1, 2, 3):
+            tell(everyone, dx, 0)
 
     with jax.named_scope("wait_green"):
         pltpu.make_async_copy(green_all.at[others], green_all.at[others], green_recv).wait()
@@ -193,15 +232,16 @@
     with jax.named_scope("spectra"):
 
         def product(k, _):
-            rows = pl.ds(pl.multiple_of(8 * k, 8), 8)
-            spectra[rows, :] = jnp.dot(
+            rows = pl.ds(pl.multiple_of(16 * k, 16), 16)
+            both = jnp.dot(
                 jnp.concatenate([lhs[0, rows, :], lhs[1, rows, :]], axis=1).astype(bf16),
-                phasors[k],
+                jnp.concatenate([phasors[2 * k], phasors[2 * k + 1]], axis=1),
                 preferred_element_type=f32,
             )
+            spectra[rows, :] = jnp.concatenate([both[:8, :128], both[8:, 128:]], axis=0)
             return 0
 
-        lax.fori_loop(0, STEPS, product, 0, unroll=8)
+        lax.fori_loop(0, STEPS // 2, product, 0, unroll=4)
 
     with jax.named_scope("turn"):
         low = lax.broadcasted_iota(jnp.int32, (64, 128), 1) < 64
@@ -217,9 +257,12 @@
                     WORKERS * c : WORKERS * c + WORKERS
                 ]
 
+    with jax.named_scope("all_here"):
+        pl.semaphore_wait(everyone, 3)
+
     with jax.named_scope("send_sums"):
-        for i in range(1, WORKERS):
-            to = (worker + i) % WORKERS
+        for dx, dz in STEPS_TO:
+            to = (x + dx) % (WORKERS // LINE) * LINE + (z + dz) % LINE
             copy = pltpu.make_async_remote_copy(
                 src_ref=partial.at[pl.ds(pl.multiple_of(8 * to, 8), 8)],
                 dst_ref=arrived.at[worker],
@@ -231,7 +274,6 @@
             copy.start()
         arrived[worker] = partial[pl.ds(pl.multiple_of(8 * worker, 8), 8), :]
     with jax.named_scope("wait_sums"):
-        most = pl.ds(0, WORKERS - 1)
         pltpu.make_async_copy(arrived.at[most], arrived.at[most], sum_recv).wait()
 
     with jax.named_scope("half"):
@@ -248,7 +290,7 @@
             device_id_type=MESH,
         )
         copy.start()
-        copy.wait()
+        copy.wait_recv()
 
     with jax.named_scope("weigh"):
         real, imag = [], []
@@ -289,13 +331,14 @@
             peaks[worker, r : r + 1, :] = top[:, 128 * r : 128 * r + 128]
 
     with jax.named_scope("send_peaks"):
-        for i in range(1, WORKERS):
+        for dx, dz in STEPS_TO:
+            to = (x + dx) % (WORKERS // LINE) * LINE + (z + dz) % LINE
             copy = pltpu.make_async_remote_copy(
                 src_ref=peaks.at[worker],
                 dst_ref=peaks.at[worker],
                 send_sem=peak_send,
                 recv_sem=peak_recv,
-                device_id={"worker": (worker + i) % WORKERS},
+                device_id={"worker": to},
                 device_id_type=MESH,
             )
             copy.start()
@@ -314,6 +357,7 @@
         pltpu.make_async_copy(field_all.at[others], field_all.at[others], field_send).wait()
         pltpu.make_async_copy(green_all.at[others], green_all.at[others], green_send).wait()
         pltpu.make_async_copy(arrived.at[most], arrived.at[most], sum_send).wait()
+        pltpu.make_async_copy(halves.at[core], halves.at[core], half_send).wait()
         pltpu.make_async_copy(peaks.at[most], peaks.at[most], peak_send).wait()
 
 
@@ -323,15 +367,14 @@
     return pl.pallas_call(
         kernel,
         out_shape=jax.ShapeDtypeStruct((MOST, 2 * NP), f32),
-        in_specs=[
-            vmem,
-            vmem,
-            vmem,
-            vmem,
-            pl.BlockSpec(memory_space=pltpu.SMEM),
-        ],
+        in_specs=[pl.BlockSpec(memory_space=pltpu.HBM)] * 5,
         out_specs=vmem,
         scratch_shapes=[
+            pltpu.VMEM((ROWS, 4 * NF), bf16),
+            pltpu.VMEM((ROWS, NP), f32),
+            pltpu.VMEM((ROWS, NP), f32),
+            pltpu.VMEM((1, NP), f32),
+            pltpu.SMEM((GROUPS * WORKERS,), jnp.int32),
             pltpu.VMEM((2, TIMES, NF), bf16),
             pltpu.VMEM((2, ROWS, 4 * HALF), f32),
             pltpu.VMEM((GROUPS // 2, ROWS, 128), f32),
@@ -347,17 +390,24 @@
             pltpu.VMEM((2, NP, NF), f32),
             pltpu.VMEM((MOST, WORKERS, 4, 128), f32),
         ]
-        + [dma] * 10,
+        + [dma((5,))]
+        + [dma] * 10
+        + [pltpu.SemaphoreType.REGULAR] * 3,
         compiler_params=pltpu.CompilerParams(
             collective_id=0, has_side_effects=True, vmem_limit_bytes=32 * 1024 * 1024
         ),
         name="seismogram",
     )(
-        green_tensor,
-        slip_field,
-        rupture_time,
-        periods.reshape(1, NP),
-        owner_map.reshape(-1),
+        *(
+            pltpu.with_memory_space_constraint(x, pltpu.HBM)
+            for x in (
+                green_tensor,
+                slip_field,
+                rupture_time,
+                periods.reshape(1, NP),
+                owner_map.reshape(-1),
+            )
+        )
     )
 
 

time: 39.1 us -> 30.9 us (0.79)
  Pallas kernels: 35.4 us -> 30.2 us
  local copies, waits for them, and re-layouts: 3.49 us -> 0.6 us
    pallas_call x1, Pallas kernels: 35.4 us -> 30.2 us  [local(): pl.pallas_call(kernel, out_shape=jax.ShapeDtypeStruct((MOST, 2 * NP), f32...]
    unnamed x11 -> x1, local copies, waits for them, and re-layouts: 3.49 us -> 0.6 us
where the time goes in v2:
time: 30.9 us; the launch traced here: 30.8 us
  Pallas kernels  30.2 us (98%)
  local copies, waits for them, and re-layouts  0.6 us (2%)
    pallas_call x1, Pallas kernels, local(): pl.pallas_call(kernel, out_shape=jax.ShapeDtypeStruct((MOST, 2 * NP), f32...  30.2 us

profile of v2, /device:TPU:1, one launch (start us, length us, event | category | flops | bytes accessed | tf_op | source)
XLA Modules:
  0.0 30.8 jit_solution(16585873477003159378)
XLA Ops:
  0.0 30.2 %seismogram.1 = f32[3,512]{1,0:T(4,128)S(1)} custom-call(bf16[16,1024]{1,0:T(8,128)(2,1)} %green_hbm.1, f32[16,256]{1,0:T(8,128)} %slip_hbm.1, f32[16,256]{1,0:T(8,128)} %time_hbm.1, f32[1,256]{1,0:T(1,128)} %bitcast.2, s32[256]{0:T(256)} %bitcast.3), custom_call_target="tpu_custom_call" | custom-call | tf_op jit(solution)/shard_map/seismogram/pallas_call | solution.py:367
  30.2 0.6 %copy.7 = f32[3,512]{1,0:T(4,128)} copy(f32[3,512]{1,0:T(4,128)S(1)} %seismogram.1) | data formatting | bytes 12288

commit v3 on v2

v3 whole, which is shorter than its diff:
```python
import functools
import math

import jax
import jax.numpy as jnp
from jax import lax
from jax.experimental import pallas as pl
from jax.experimental.pallas import tpu as pltpu
from jax.sharding import PartitionSpec as P

NT = 4096
NF = 256
NP = 256
MOST = 3
TIME_STEP = 0.05
DAMPING = 0.05

GROUPS = 8
WORKERS = 32
LINE = 8
ROWS = 16
ORDER = [
    (j, x * LINE + z) for zs in ((0, 1, 2, 3, 7, 6, 5, 4),) for j in range(MOST) for z in zs for x in (0, 1, 3, 2)
]

PARTNERS = 16
GATHERED = ROWS * PARTNERS
QUARTER = 64
STEPS = 32
TIMES = NT // 2 + 16
BLOCKS = [(0, 512), (512, 512), (1024, 512), (1536, 528)]

f32 = jnp.float32
bf16 = jnp.bfloat16
MESH = pl.DeviceIdType.MESH


def cos_sin_turns(turns):
    near = turns - jnp.round(turns)
    angle = near * (2.0 * math.pi)
    square = angle * angle
    cos = f32(0.0)
    for n in range(8, -1, -1):
        cos = cos * square + f32((-1) ** n / math.factorial(2 * n))
    sin = f32(0.0)
    for n in range(8, -1, -1):
        sin = sin * square + f32((-1) ** n / math.factorial(2 * n + 1))
    return cos, sin * angle


def kernel(
    green_hbm, slip_hbm, time_hbm, periods_hbm, owner_hbm, out_ref,
    green_ref, slip_ref, time_ref, periods_ref, owner_ref, basis, green_stage, field_stage, green_all, field_all, phasors, lhs, spectra,
    partial, arrived, gain, chosen,
    load_sem, field_send, field_recv, green_send, green_recv,
    sum_send, sum_recv,
    near, line, everyone,
):
    group = lax.axis_index("group")
    worker = lax.axis_index("worker")
    row, core = group // 2, group % 2

    x, z = worker // LINE, worker % LINE

    def tell(semaphore, dx, dz):
        to = (x + dx) % (WORKERS // LINE) * LINE + (z + dz) % LINE
        pl.semaphore_signal(semaphore, inc=1, device_id={"worker": to}, device_id_type=MESH)

    place = z % 2
    me = 2 * group + place

    def partner(i):
        return {"group": i // 2, "worker": worker - place + i % 2}

    barrier = pltpu.get_barrier_semaphore()
    for i in range(1, PARTNERS):
        pl.semaphore_signal(
            barrier, inc=1, device_id=partner((me + i) % PARTNERS), device_id_type=MESH
        )
    loads = [
        pltpu.make_async_copy(source, target, load_sem.at[i])
        for i, (source, target) in enumerate(
            [
                (slip_hbm, slip_ref),
                (time_hbm, time_ref),
                (green_hbm, green_ref),
                (periods_hbm, periods_ref),
                (owner_hbm, owner_ref),
            ]
        )
    ]
    for load in loads:
        load.start()
    for dx, dz in ((0, 1), (0, -1), (1, 0), (-1, 0)):
        tell(barrier, dx, dz)

    for load in loads[:3]:
        load.wait()
    with jax.named_scope("stage"):
        for y in range(GROUPS // 2):
            lanes = slice(64 * y, 64 * y + 64)
            field_stage[y] = jnp.concatenate([slip_ref[:, lanes], time_ref[:, lanes]], axis=1)
        for part in range(4):
            for quarter in range(4):
                start = part * NF + quarter * QUARTER
                green_stage[quarter, :, part * QUARTER : (part + 1) * QUARTER] = green_ref[
                    :, start : start + QUARTER
                ].astype(f32)

    with jax.named_scope("barrier"):
        pl.semaphore_wait(barrier, PARTNERS - 1 + 4)

    others = pl.ds(0, ROWS * (PARTNERS - 1))
    mine = pl.ds(pl.multiple_of(ROWS * me, ROWS), ROWS)
    with jax.named_scope("send_fields"):
        for to in range(PARTNERS):
            copy = pltpu.make_async_remote_copy(
                src_ref=field_stage.at[to // 4],
                dst_ref=field_all.at[mine],
                send_sem=field_send,
                recv_sem=field_recv,
                device_id=partner(to),
                device_id_type=MESH,
            )
            pl.when(me != to)(copy.start)
        for dx, dz in ((0, 1), (0, -1), (1, 0), (-1, 0)):
            tell(near, dx, dz)
        for to in range(PARTNERS):
            copy = pltpu.make_async_remote_copy(
                src_ref=green_stage.at[to % 4],
                dst_ref=green_all.at[mine],
                send_sem=green_send,
                recv_sem=green_recv,
                device_id=partner(to),
                device_id_type=MESH,
            )
            pl.when(me != to)(copy.start)
    field_all[mine, :] = field_stage[row]
    green_all[mine, :] = green_stage[2 * core + place]

    for load in loads[3:]:
        load.wait()
    with jax.named_scope("gain"):
        natural = (2.0 * math.pi) / periods_ref[...]
        column = jnp.concatenate(
            [
                jnp.transpose(jnp.broadcast_to(natural[:, :128], (128, 128))),
                jnp.transpose(jnp.broadcast_to(natural[:, 128:], (128, 128))),
            ],
            axis=0,
        )
        for h in range(2):
            index = lax.broadcasted_iota(jnp.int32, (NP, 128), 1) + 128 * h
            angular = (2.0 * math.pi) * index.astype(f32) / (NT * TIME_STEP)
            denom_real = column * column - angular * angular
            denom_imag = (2.0 * DAMPING) * column * angular
            scale = column * column / (denom_real * denom_real + denom_imag * denom_imag)
            gain[0, :, 128 * h : 128 * h + 128] = -scale * denom_real
            gain[1, :, 128 * h : 128 * h + 128] = scale * denom_imag

    with jax.named_scope("basis"):
        freq = lax.broadcasted_iota(jnp.int32, (16, NF), 1)
        time = lax.broadcasted_iota(jnp.int32, (16, NF), 0)
        fold = jnp.where(freq == 0, 1.0, 2.0)
        cos0, sin0 = cos_sin_turns((freq * time).astype(f32) * (1.0 / NT))
        cos16, sin16 = cos_sin_turns(freq.astype(f32) * (16.0 / NT))

        def advance(b, carry):
            cos, sin = carry
            rows = pl.ds(pl.multiple_of(16 * b, 16), 16)
            basis[0, rows, :] = cos.astype(bf16)
            basis[1, rows, :] = sin.astype(bf16)
            return cos * cos16 + sin * sin16, sin * cos16 - cos * sin16

        lax.fori_loop(0, TIMES // 16, advance, (fold * cos0, -fold * sin0), unroll=3)

    with jax.named_scope("owners"):
        pair = owner_ref[:, 0:64]
        for y in range(1, GROUPS // 2):
            pair = jnp.where(row == y, owner_ref[:, 64 * y : 64 * y + 64], pair)
        pair = jnp.concatenate([pair, pair], axis=1)
        lane = lax.broadcasted_iota(jnp.int32, (128, 128), 1) % 64
        other = lax.broadcasted_iota(jnp.int32, (128, 128), 0)
        named = jnp.broadcast_to(pair, (128, 128))
        same = (jnp.transpose(named) == named) & (other // WORKERS == lane // WORKERS)
        earlier = jnp.where(same & (other < lane), 1.0, 0.0)
        rank = jnp.sum(earlier, axis=0, keepdims=True).astype(jnp.int32)
        for j in range(MOST):
            for c in range(2):
                lane = lax.broadcasted_iota(jnp.int32, (WORKERS, 128), 1) % 64
                owner = lax.broadcasted_iota(jnp.int32, (WORKERS, 128), 0)
                hit = (pair == owner) & (lane // WORKERS == c) & (rank == j)
                start = (2 * j + c) * WORKERS
                chosen[start : start + WORKERS, :] = jnp.where(hit, 1.0, 0.0).astype(bf16)

    with jax.named_scope("along_z"):
        pl.semaphore_wait(near, 4)
        for dz in (2, -2):
            tell(line, 0, dz)

    with jax.named_scope("wait_fields"):
        pltpu.make_async_copy(field_all.at[others], field_all.at[others], field_recv).wait()

    with jax.named_scope("phasors"):
        for s in range(0, GATHERED, 32):
            field = field_all[s : s + 32, :]
            swapped = pltpu.roll(field, 64, 1)
            lane = lax.broadcasted_iota(jnp.int32, (32, 128), 1)
            low = lane < 64
            slip = jnp.where(low, field, swapped)
            turn = jnp.where(low, swapped, field) * (1.0 / (NT * TIME_STEP))
            first = ((2 * core + place) * QUARTER + jnp.where(low, 0, STEPS)).astype(f32)
            cos0, sin0 = cos_sin_turns(turn * first)
            cos1, sin1 = cos_sin_turns(turn)

            def step(k, carry, s=s, cos1=cos1, sin1=sin1):
                cos, sin = carry
                phasors[k, s : s + 32, :] = cos.astype(bf16)
                phasors[k, GATHERED + s : GATHERED + s + 32, :] = sin.astype(bf16)
                return cos * cos1 - sin * sin1, sin * cos1 + cos * sin1

            lax.fori_loop(0, STEPS, step, (slip * cos0, slip * sin0), unroll=8)

    with jax.named_scope("along_x"):
        pl.semaphore_wait(line, 2)
        for dx in (1, 2, 3):
            tell(everyone, dx, 0)

    with jax.named_scope("wait_green"):
        pltpu.make_async_copy(green_all.at[others], green_all.at[others], green_recv).wait()

    with jax.named_scope("green"):
        for c in range(2):
            for half in range(2):
                turned = jnp.transpose(
                    green_all[128 * half : 128 * half + 128, 128 * c : 128 * c + 128]
                )
                for h in range(2):
                    value = [
                        turned[QUARTER * part + STEPS * h : QUARTER * part + STEPS * h + STEPS, :]
                        for part in range(2)
                    ]
                    real = pl.ds(4 * h + 2 * c, STEPS, stride=8)
                    imag = pl.ds(4 * h + 2 * c + 1, STEPS, stride=8)
                    lhs[half, real, :] = value[0]
                    lhs[half, imag, :] = value[1]
                    lhs[2 + half, real, :] = value[1]
                    lhs[2 + half, imag, :] = -value[0]

    with jax.named_scope("spectra"):

        def product(k, _):
            rows = pl.ds(pl.multiple_of(16 * k, 16), 16)
            both = jnp.dot(
                jnp.concatenate([lhs[i, rows, :] for i in range(4)], axis=1).astype(bf16),
                jnp.concatenate([phasors[2 * k], phasors[2 * k + 1]], axis=1),
                preferred_element_type=f32,
            )
            spectra[rows, :] = jnp.concatenate([both[:8, :128], both[8:, 128:]], axis=0)
            return 0

        lax.fori_loop(0, STEPS // 2, product, 0, unroll=4)

    contract = (((1,), (1,)), ((), ()))
    with jax.named_scope("place"):
        low = lax.broadcasted_iota(jnp.int32, (STEPS, 128), 1) < 64
        for c in range(2):
            parts = []
            for r in (2 * c, 2 * c + 1):
                parts.append(jnp.where(low, spectra[pl.ds(r, STEPS, stride=8), :], 0.0))
                parts.append(jnp.where(low, 0.0, spectra[pl.ds(4 + r, STEPS, stride=8), :]))
            rest = jnp.concatenate(parts, axis=0)
            value = jnp.zeros((2 * MOST * WORKERS, 128), f32)
            for _ in range(3):
                piece = rest.astype(bf16)
                rest = rest - piece.astype(f32)
                value = value + lax.dot_general(
                    chosen[...], piece, contract, preferred_element_type=f32
                )
            for block in range(2 * MOST):
                partial[pl.ds(2 * WORKERS * block + c, WORKERS, stride=2), :] = value[
                    WORKERS * block : WORKERS * block + WORKERS
                ]

    with jax.named_scope("all_here"):
        pl.semaphore_wait(everyone, 3)

    def part(j, c, w):
        return pl.ds(pl.multiple_of(2 * (WORKERS * (2 * j + c) + w), 2), 2)

    with jax.named_scope("send_sums"):
        for j, to in ORDER:
            for c in (1, 0):
                copy = pltpu.make_async_remote_copy(
                    src_ref=partial.at[part(j, c, to)],
                    dst_ref=arrived.at[j, part(0, core, worker)],
                    send_sem=sum_send,
                    recv_sem=sum_recv.at[j],
                    device_id={"group": 2 * row + c, "worker": to},
                    device_id_type=MESH,
                )
                pl.when((worker != to) | (core != c))(copy.start)
        for j in range(MOST):
            arrived[j, part(0, core, worker), :] = partial[part(j, core, worker), :]

    most = pl.ds(0, 2 * (2 * WORKERS - 1))
    for j in range(MOST):
        with jax.named_scope("wait_sums"):
            pltpu.make_async_copy(
                arrived.at[j, most], arrived.at[j, most], sum_recv.at[j]
            ).wait()

        with jax.named_scope("weigh"):
            spec = []
            for h in range(2):
                total = arrived[j, 2 * WORKERS * h : 2 * WORKERS * h + 8, :]
                for i in range(8, 2 * WORKERS, 8):
                    total = total + arrived[j, 2 * WORKERS * h + i : 2 * WORKERS * h + i + 8, :]
                spec.append(total[:4] + total[4:])
            real, imag = [], []
            for c in range(2):
                for h in range(2):
                    near_part, far_part = spec[h][c : c + 1], spec[h][2 + c : 3 + c]
                    spec_real = jnp.concatenate([near_part[:, :64], far_part[:, :64]], axis=1)
                    spec_imag = jnp.concatenate([near_part[:, 64:], far_part[:, 64:]], axis=1)
                    gain_real = gain[0, :, 128 * h : 128 * h + 128]
                    gain_imag = gain[1, :, 128 * h : 128 * h + 128]
                    real.append((spec_real * gain_real - spec_imag * gain_imag).astype(bf16))
                    imag.append((spec_real * gain_imag + spec_imag * gain_real).astype(bf16))
            weighted = [
                [jnp.concatenate(v[2 * c : 2 * c + 2], axis=1) for v in (real, imag)]
                for c in range(2)
            ]

        with jax.named_scope("response"):
            for c in range(2):
                best = jnp.zeros((8, NP), f32)
                for start, size in BLOCKS:
                    even, odd = [
                        lax.dot_general(
                            basis[i, start : start + size, :],
                            weighted[c][i],
                            contract,
                            preferred_element_type=f32,
                        )
                        for i in range(2)
                    ]
                    value = jnp.abs(even) + jnp.abs(odd)
                    for t in range(0, size, 8):
                        best = jnp.maximum(best, value[t : t + 8])
                top = jnp.max(best, axis=0, keepdims=True) * (1.0 / math.sqrt(NF))
                out_ref[j : j + 1, NP * c : NP * c + NP] = top

    with jax.named_scope("wait_sent"):
        pltpu.make_async_copy(field_all.at[others], field_all.at[others], field_send).wait()
        pltpu.make_async_copy(green_all.at[others], green_all.at[others], green_send).wait()
        for j in range(MOST):
            pltpu.make_async_copy(arrived.at[j, most], arrived.at[j, most], sum_send).wait()


def local(green_tensor, slip_field, rupture_time, periods, owner_map):
    vmem = pl.BlockSpec(memory_space=pltpu.VMEM)
    dma = pltpu.SemaphoreType.DMA
    return pl.pallas_call(
        kernel,
        out_shape=jax.ShapeDtypeStruct((MOST, 2 * NP), f32),
        in_specs=[pl.BlockSpec(memory_space=pltpu.HBM)] * 5,
        out_specs=vmem,
        scratch_shapes=[
            pltpu.VMEM((ROWS, 4 * NF), bf16),
            pltpu.VMEM((ROWS, NP), f32),
            pltpu.VMEM((ROWS, NP), f32),
            pltpu.VMEM((1, NP), f32),
            pltpu.VMEM((1, GROUPS * WORKERS), jnp.int32),
            pltpu.VMEM((2, TIMES, NF), bf16),
            pltpu.VMEM((4, ROWS, 4 * QUARTER), f32),
            pltpu.VMEM((GROUPS // 2, ROWS, 128), f32),
            pltpu.VMEM((GATHERED, 4 * QUARTER), f32),
            pltpu.VMEM((GATHERED, 128), f32),
            pltpu.VMEM((STEPS, 2 * GATHERED, 128), bf16),
            pltpu.VMEM((4, 8 * STEPS, 128), f32),
            pltpu.VMEM((8 * STEPS, 128), f32),
            pltpu.VMEM((2 * 2 * MOST * WORKERS, 128), f32),
            pltpu.VMEM((MOST, 2 * 2 * WORKERS, 128), f32),
            pltpu.VMEM((2, NP, NF), f32),
            pltpu.VMEM((2 * MOST * WORKERS, 128), bf16),
        ]
        + [dma((5,))]
        + [dma] * 5 + [dma((MOST,))]
        + [pltpu.SemaphoreType.REGULAR] * 3,
        compiler_params=pltpu.CompilerParams(
            collective_id=0, has_side_effects=True, vmem_limit_bytes=32 * 1024 * 1024
        ),
        name="seismogram",
    )(
        *(
            pltpu.with_memory_space_constraint(x, pltpu.HBM)
            for x in (
                green_tensor,
                slip_field,
                rupture_time,
                periods.reshape(1, NP),
                owner_map.reshape(1, -1),
            )
        )
    )


def solution(mesh):
    placed = (
        P(("group", "worker"), None),
        P(("group", "worker"), None),
        P(("group", "worker"), None),
        P(),
        P(),
    )
    return jax.shard_map(
        local, mesh=mesh, in_specs=placed, out_specs=P(("group", "worker"), None), check_vma=False
    )
```

time: 30.9 us -> 29.8 us (0.964)
  Pallas kernels: 30.2 us -> 29.1 us
    pallas_call x1, Pallas kernels: 30.2 us -> 29.1 us  [local(): pl.pallas_call(kernel, out_shape=jax.ShapeDtypeStruct((MOST, 2 * NP), f32...]
where the time goes in v3:
time: 29.8 us; the launch traced here: 29.7 us
  Pallas kernels  29.1 us (98%)
  local copies, waits for them, and re-layouts  0.6 us (2%)
    pallas_call x1, Pallas kernels, local(): pl.pallas_call(kernel, out_shape=jax.ShapeDtypeStruct((MOST, 2 * NP), f32...  29.1 us
    unnamed x1, local copies, waits for them, and re-layouts  0.6 us

profile of v3, /device:TPU:1, one launch (start us, length us, event | category | flops | bytes accessed | tf_op | source)
XLA Modules:
  0.0 29.7 jit_solution(3375693840071624708)
XLA Ops:
  0.0 29.1 %seismogram.1 = f32[3,512]{1,0:T(4,128)S(1)} custom-call(bf16[16,1024]{1,0:T(8,128)(2,1)} %green_hbm.1, f32[16,256]{1,0:T(8,128)} %slip_hbm.1, f32[16,256]{1,0:T(8,128)} %time_hbm.1, f32[1,256]{1,0:T(1,128)} %bitcast.2, s32[1,256]{1,0:T(1,128)} %bitcast.3), custom_call_target="tpu_custom_call" | custom-call | tf_op jit(solution)/shard_map/seismogram/pallas_call | solution.py:364
  29.1 0.6 %copy.7 = f32[3,512]{1,0:T(4,128)} copy(f32[3,512]{1,0:T(4,128)S(1)} %seismogram.1) | data formatting | bytes 12288

commit v4 on v3

--- a/solution.py
+++ b/solution.py
@@ -19,12 +19,20 @@
 WORKERS = 32
 LINE = 8
 ROWS = 16
+EXTRA = (MOST - 1, 0, 1)
 ORDER = [
-    (j, x * LINE + z) for zs in ((0, 1, 2, 3, 7, 6, 5, 4),) for j in range(MOST) for z in zs for x in (0, 1, 3, 2)
+    (j, x * LINE + z, c)
+    for j in range(MOST)
+    for z in (0, 1, 2, 3, 7, 6, 5, 4)
+    for x in (0, 1, 3, 2)
+    for c in (1, 0)
 ]
-
+ORDER.remove(EXTRA)
+ORDER.insert(1, EXTRA)
 PARTNERS = 16
 GATHERED = ROWS * PARTNERS
+BAND = 64
+UNROLL = 8
 QUARTER = 64
 STEPS = 32
 TIMES = NT // 2 + 16
@@ -51,9 +59,9 @@
 def kernel(
     green_hbm, slip_hbm, time_hbm, periods_hbm, owner_hbm, out_ref,
     green_ref, slip_ref, time_ref, periods_ref, owner_ref, basis, green_stage, field_stage, green_all, field_all, phasors, lhs, spectra,
-    partial, arrived, gain, chosen,
+    partial, arrived, gain, chosen, given,
     load_sem, field_send, field_recv, green_send, green_recv,
-    sum_send, sum_recv,
+    sum_send, sum_recv, give_send, give_recv,
     near, line, everyone,
 ):
     group = lax.axis_index("group")
@@ -67,6 +75,8 @@
         pl.semaphore_signal(semaphore, inc=1, device_id={"worker": to}, device_id_type=MESH)
 
     place = z % 2
+    helped = (row == 0) & (worker == 0) & (core == 1)
+    helper = (row == 0) & (worker == 0) & (core == 0)
     me = 2 * group + place
 
     def partner(i):
@@ -110,15 +120,20 @@
     with jax.named_scope("barrier"):
         pl.semaphore_wait(barrier, PARTNERS - 1 + 4)
 
-    others = pl.ds(0, ROWS * (PARTNERS - 1))
-    mine = pl.ds(pl.multiple_of(ROWS * me, ROWS), ROWS)
+    own = pl.ds(pl.multiple_of(ROWS * (2 * core + place), ROWS), ROWS)
+
+    def spot(to):
+        away = (row - to // 4 + 4) % 4
+        return away + away // 2 * (5 - 2 * away)
+
     with jax.named_scope("send_fields"):
         for to in range(PARTNERS):
+            rows = pl.ds(pl.multiple_of(BAND * spot(to) + ROWS * (2 * core + place), ROWS), ROWS)
             copy = pltpu.make_async_remote_copy(
                 src_ref=field_stage.at[to // 4],
-                dst_ref=field_all.at[mine],
+                dst_ref=field_all.at[rows],
                 send_sem=field_send,
-                recv_sem=field_recv,
+                recv_sem=field_recv.at[spot(to)],
                 device_id=partner(to),
                 device_id_type=MESH,
             )
@@ -126,17 +141,18 @@
         for dx, dz in ((0, 1), (0, -1), (1, 0), (-1, 0)):
             tell(near, dx, dz)
         for to in range(PARTNERS):
+            rows = pl.ds(pl.multiple_of(BAND * spot(to) + ROWS * (2 * core + place), ROWS), ROWS)
             copy = pltpu.make_async_remote_copy(
                 src_ref=green_stage.at[to % 4],
-                dst_ref=green_all.at[mine],
+                dst_ref=green_all.at[rows],
                 send_sem=green_send,
-                recv_sem=green_recv,
+                recv_sem=green_recv.at[spot(to) // 2],
                 device_id=partner(to),
                 device_id_type=MESH,
             )
             pl.when(me != to)(copy.start)
-    field_all[mine, :] = field_stage[row]
-    green_all[mine, :] = green_stage[2 * core + place]
+    field_all[own, :] = field_stage[row]
+    green_all[own, :] = green_stage[2 * core + place]
 
     for load in loads[3:]:
         load.wait()
@@ -198,40 +214,48 @@
         for dz in (2, -2):
             tell(line, 0, dz)
 
-    with jax.named_scope("wait_fields"):
-        pltpu.make_async_copy(field_all.at[others], field_all.at[others], field_recv).wait()
-
-    with jax.named_scope("phasors"):
-        for s in range(0, GATHERED, 32):
-            field = field_all[s : s + 32, :]
-            swapped = pltpu.roll(field, 64, 1)
-            lane = lax.broadcasted_iota(jnp.int32, (32, 128), 1)
-            low = lane < 64
-            slip = jnp.where(low, field, swapped)
-            turn = jnp.where(low, swapped, field) * (1.0 / (NT * TIME_STEP))
-            first = ((2 * core + place) * QUARTER + jnp.where(low, 0, STEPS)).astype(f32)
-            cos0, sin0 = cos_sin_turns(turn * first)
-            cos1, sin1 = cos_sin_turns(turn)
-
-            def step(k, carry, s=s, cos1=cos1, sin1=sin1):
-                cos, sin = carry
-                phasors[k, s : s + 32, :] = cos.astype(bf16)
-                phasors[k, GATHERED + s : GATHERED + s + 32, :] = sin.astype(bf16)
-                return cos * cos1 - sin * sin1, sin * cos1 + cos * sin1
-
-            lax.fori_loop(0, STEPS, step, (slip * cos0, slip * sin0), unroll=8)
+    for band in range(4):
+        with jax.named_scope("wait_fields"):
+            arriving = pl.ds(BAND * band, BAND - ROWS if band == 0 else BAND)
+            pltpu.make_async_copy(
+                field_all.at[arriving], field_all.at[arriving], field_recv.at[band]
+            ).wait()
+
+        with jax.named_scope("phasors"):
+            for s in range(BAND * band, BAND * band + BAND, 32):
+                field = field_all[s : s + 32, :]
+                swapped = pltpu.roll(field, 64, 1)
+                lane = lax.broadcasted_iota(jnp.int32, (32, 128), 1)
+                low = lane < 64
+                slip = jnp.where(low, field, swapped)
+                turn = jnp.where(low, swapped, field) * (1.0 / (NT * TIME_STEP))
+                first = ((2 * core + place) * QUARTER + jnp.where(low, 0, STEPS)).astype(f32)
+                cos0, sin0 = cos_sin_turns(turn * first)
+                cos1, sin1 = cos_sin_turns(turn)
+                at = s + s // 128 * 128
+
+                def step(k, carry, at=at, cos1=cos1, sin1=sin1):
+                    cos, sin = carry
+                    phasors[k, at : at + 32, :] = cos.astype(bf16)
+                    phasors[k, at + 128 : at + 160, :] = sin.astype(bf16)
+                    return cos * cos1 - sin * sin1, sin * cos1 + cos * sin1
+
+                lax.fori_loop(0, STEPS, step, (slip * cos0, slip * sin0), unroll=8)
 
     with jax.named_scope("along_x"):
         pl.semaphore_wait(line, 2)
         for dx in (1, 2, 3):
             tell(everyone, dx, 0)
 
-    with jax.named_scope("wait_green"):
-        pltpu.make_async_copy(green_all.at[others], green_all.at[others], green_recv).wait()
-
-    with jax.named_scope("green"):
-        for c in range(2):
-            for half in range(2):
+    for half in range(2):
+        with jax.named_scope("wait_green"):
+            arriving = pl.ds(128 * half, 128 - ROWS if half == 0 else 128)
+            pltpu.make_async_copy(
+                green_all.at[arriving], green_all.at[arriving], green_recv.at[half]
+            ).wait()
+
+        with jax.named_scope("green"):
+            for c in range(2):
                 turned = jnp.transpose(
                     green_all[128 * half : 128 * half + 128, 128 * c : 128 * c + 128]
                 )
@@ -242,24 +266,30 @@
                     ]
                     real = pl.ds(4 * h + 2 * c, STEPS, stride=8)
                     imag = pl.ds(4 * h + 2 * c + 1, STEPS, stride=8)
-                    lhs[half, real, :] = value[0]
-                    lhs[half, imag, :] = value[1]
-                    lhs[2 + half, real, :] = value[1]
-                    lhs[2 + half, imag, :] = -value[0]
-
-    with jax.named_scope("spectra"):
-
-        def product(k, _):
-            rows = pl.ds(pl.multiple_of(16 * k, 16), 16)
-            both = jnp.dot(
-                jnp.concatenate([lhs[i, rows, :] for i in range(4)], axis=1).astype(bf16),
-                jnp.concatenate([phasors[2 * k], phasors[2 * k + 1]], axis=1),
-                preferred_element_type=f32,
-            )
-            spectra[rows, :] = jnp.concatenate([both[:8, :128], both[8:, 128:]], axis=0)
-            return 0
-
-        lax.fori_loop(0, STEPS // 2, product, 0, unroll=4)
+                    lhs[2 * half, real, :] = value[0]
+                    lhs[2 * half, imag, :] = value[1]
+                    lhs[2 * half + 1, real, :] = value[1]
+                    lhs[2 * half + 1, imag, :] = -value[0]
+
+        with jax.named_scope("spectra"):
+
+            def product(k, _, half=half):
+                rows = pl.ds(pl.multiple_of(16 * k, 16), 16)
+                depth = slice(256 * half, 256 * half + 256)
+                both = jnp.dot(
+                    jnp.concatenate([lhs[2 * half + i, rows, :] for i in range(2)], axis=1).astype(
+                        bf16
+                    ),
+                    jnp.concatenate(
+                        [phasors[2 * k, depth, :], phasors[2 * k + 1, depth, :]], axis=1
+                    ),
+                    preferred_element_type=f32,
+                )
+                value = jnp.concatenate([both[:8, :128], both[8:, 128:]], axis=0)
+                spectra[rows, :] = value if half == 0 else spectra[rows, :] + value
+                return 0
+
+            lax.fori_loop(0, STEPS // 2, product, 0, unroll=UNROLL)
 
     contract = (((1,), (1,)), ((), ()))
     with jax.named_scope("place"):
@@ -289,22 +319,29 @@
         return pl.ds(pl.multiple_of(2 * (WORKERS * (2 * j + c) + w), 2), 2)
 
     with jax.named_scope("send_sums"):
-        for j, to in ORDER:
-            for c in (1, 0):
-                copy = pltpu.make_async_remote_copy(
-                    src_ref=partial.at[part(j, c, to)],
-                    dst_ref=arrived.at[j, part(0, core, worker)],
-                    send_sem=sum_send,
-                    recv_sem=sum_recv.at[j],
-                    device_id={"group": 2 * row + c, "worker": to},
-                    device_id_type=MESH,
-                )
-                pl.when((worker != to) | (core != c))(copy.start)
+        for j, to, c in ORDER:
+            slot, source = j, partial.at[part(j, c, to)]
+            if (j, to, c) == EXTRA:
+                aside = jnp.where(row == 0, 1, 0)
+                slot, c = j + aside, c - aside
+            copy = pltpu.make_async_remote_copy(
+                src_ref=source,
+                dst_ref=arrived.at[slot, part(0, core, worker)],
+                send_sem=sum_send,
+                recv_sem=sum_recv.at[slot],
+                device_id={"group": 2 * row + c, "worker": to},
+                device_id_type=MESH,
+            )
+            pl.when((worker != to) | (core != c))(copy.start)
         for j in range(MOST):
             arrived[j, part(0, core, worker), :] = partial[part(j, core, worker), :]
 
+        @pl.when(helper)
+        def _():
+            arrived[MOST, part(0, core, worker), :] = partial[part(MOST - 1, 1, worker), :]
+
     most = pl.ds(0, 2 * (2 * WORKERS - 1))
-    for j in range(MOST):
+    def peaks(j):
         with jax.named_scope("wait_sums"):
             pltpu.make_async_copy(
                 arrived.at[j, most], arrived.at[j, most], sum_recv.at[j]
@@ -333,6 +370,7 @@
             ]
 
         with jax.named_scope("response"):
+            tops = []
             for c in range(2):
                 best = jnp.zeros((8, NP), f32)
                 for start, size in BLOCKS:
@@ -348,14 +386,47 @@
                     value = jnp.abs(even) + jnp.abs(odd)
                     for t in range(0, size, 8):
                         best = jnp.maximum(best, value[t : t + 8])
-                top = jnp.max(best, axis=0, keepdims=True) * (1.0 / math.sqrt(NF))
-                out_ref[j : j + 1, NP * c : NP * c + NP] = top
+                tops.append(jnp.max(best, axis=0, keepdims=True) * (1.0 / math.sqrt(NF)))
+        return jnp.concatenate(tops, axis=1)
+
+    give = pltpu.make_async_remote_copy(
+        src_ref=given,
+        dst_ref=given,
+        send_sem=give_send,
+        recv_sem=give_recv,
+        device_id={"group": 2 * row + 1 - core},
+        device_id_type=MESH,
+    )
+
+    @pl.when(helper)
+    def _():
+        given[...] = peaks(MOST)
+        give.start()
+
+    for j in range(MOST - 1):
+        out_ref[j : j + 1, :] = peaks(j)
+
+    @pl.when(jnp.logical_not(helped))
+    def _():
+        out_ref[MOST - 1 : MOST, :] = peaks(MOST - 1)
+
+    @pl.when(helped)
+    def _():
+        give.wait_recv()
+        out_ref[MOST - 1 : MOST, :] = given[...]
 
     with jax.named_scope("wait_sent"):
+        others = pl.ds(0, ROWS * (PARTNERS - 1))
         pltpu.make_async_copy(field_all.at[others], field_all.at[others], field_send).wait()
         pltpu.make_async_copy(green_all.at[others], green_all.at[others], green_send).wait()
-        for j in range(MOST):
+        for j in range(MOST - 1):
             pltpu.make_async_copy(arrived.at[j, most], arrived.at[j, most], sum_send).wait()
+        fewer, one = pl.ds(0, 2 * (2 * WORKERS - 2)), pl.ds(0, 2)
+        pltpu.make_async_copy(arrived.at[0, fewer], arrived.at[0, fewer], sum_send).wait()
+        last = pltpu.make_async_copy(arrived.at[0, one], arrived.at[0, one], sum_send)
+        pl.when(jnp.logical_not(helper))(last.wait)
+        pl.when(helped)(last.wait)
+        pl.when(helper)(give.wait_send)
 
 
 def local(green_tensor, slip_field, rupture_time, periods, owner_map):
@@ -381,12 +452,12 @@
             pltpu.VMEM((4, 8 * STEPS, 128), f32),
             pltpu.VMEM((8 * STEPS, 128), f32),
             pltpu.VMEM((2 * 2 * MOST * WORKERS, 128), f32),
-            pltpu.VMEM((MOST, 2 * 2 * WORKERS, 128), f32),
+            pltpu.VMEM((MOST + 1, 2 * 2 * WORKERS, 128), f32),
             pltpu.VMEM((2, NP, NF), f32),
             pltpu.VMEM((2 * MOST * WORKERS, 128), bf16),
+            pltpu.VMEM((1, 2 * NP), f32),
         ]
-        + [dma((5,))]
-        + [dma] * 5 + [dma((MOST,))]
+        + [dma((5,)), dma, dma((4,)), dma, dma((2,)), dma, dma((MOST + 1,)), dma, dma]
         + [pltpu.SemaphoreType.REGULAR] * 3,
         compiler_params=pltpu.CompilerParams(
             collective_id=0, has_side_effects=True, vmem_limit_bytes=32 * 1024 * 1024

time: 29.8 us -> 28 us (0.940); the launches traced: 29.7 us -> 27.5 us
  Pallas kernels: 29.1 us -> 26.9 us
    pallas_call x1, Pallas kernels: 29.1 us -> 26.9 us  [local(): pl.pallas_call(kernel, out_shape=jax.ShapeDtypeStruct((MOST, 2 * NP), f32...]
where the time goes in v4:
time: 28 us; the launch traced here: 27.5 us
  Pallas kernels  26.9 us (96%)
  local copies, waits for them, and re-layouts  0.6 us (2%)
    pallas_call x1, Pallas kernels, local(): pl.pallas_call(kernel, out_shape=jax.ShapeDtypeStruct((MOST, 2 * NP), f32...  26.9 us
    unnamed x1, local copies, waits for them, and re-layouts  0.6 us

profile of v4, /device:TPU:1, one launch (start us, length us, event | category | flops | bytes accessed | tf_op | source)
XLA Modules:
  0.0 27.5 jit_solution(15764490899663434484)
XLA Ops:
  0.0 26.9 %seismogram.1 = f32[3,512]{1,0:T(4,128)S(1)} custom-call(bf16[16,1024]{1,0:T(8,128)(2,1)} %green_hbm.1, f32[16,256]{1,0:T(8,128)} %slip_hbm.1, f32[16,256]{1,0:T(8,128)} %time_hbm.1, f32[1,256]{1,0:T(1,128)} %bitcast.2, s32[1,256]{1,0:T(1,128)} %bitcast.3), custom_call_target="tpu_custom_call" | custom-call | tf_op jit(solution)/shard_map/seismogram/pallas_call | solution.py:435
  26.9 0.6 %copy.7 = f32[3,512]{1,0:T(4,128)} copy(f32[3,512]{1,0:T(4,128)S(1)} %seismogram.1) | data formatting | bytes 12288

commit v5 on v4

--- a/solution.py
+++ b/solution.py
@@ -29,10 +29,13 @@
 ]
 ORDER.remove(EXTRA)
 ORDER.insert(1, EXTRA)
+SENDS = [(to, 0) for to in (0, 1, 2, 3, 12, 13, 14, 15, 8, 9, 10, 11, 4, 5, 6, 7)] + [
+    (to, 1) for to in (0, 1, 2, 3, 12, 13, 14, 15, 8, 9, 10, 11, 4, 5, 6, 7)
+]
 PARTNERS = 16
 GATHERED = ROWS * PARTNERS
 BAND = 64
-UNROLL = 8
+UNROLL = 16
 QUARTER = 64
 STEPS = 32
 TIMES = NT // 2 + 16
@@ -126,31 +129,28 @@
         away = (row - to // 4 + 4) % 4
         return away + away // 2 * (5 - 2 * away)
 
-    with jax.named_scope("send_fields"):
-        for to in range(PARTNERS):
-            rows = pl.ds(pl.multiple_of(BAND * spot(to) + ROWS * (2 * core + place), ROWS), ROWS)
-            copy = pltpu.make_async_remote_copy(
-                src_ref=field_stage.at[to // 4],
-                dst_ref=field_all.at[rows],
-                send_sem=field_send,
-                recv_sem=field_recv.at[spot(to)],
-                device_id=partner(to),
-                device_id_type=MESH,
-            )
-            pl.when(me != to)(copy.start)
+    def send(to, which):
+        rows = pl.ds(pl.multiple_of(BAND * spot(to) + ROWS * (2 * core + place), ROWS), ROWS)
+        if which == 0:
+            source, target = field_stage.at[to // 4], field_all.at[rows]
+            sent, received = field_send, field_recv.at[spot(to)]
+        else:
+            source, target = green_stage.at[to % 4], green_all.at[rows]
+            sent, received = green_send, green_recv.at[spot(to) // 2]
+        pltpu.make_async_remote_copy(
+            src_ref=source,
+            dst_ref=target,
+            send_sem=sent,
+            recv_sem=received,
+            device_id=partner(to),
+            device_id_type=MESH,
+        ).start()
+
+    with jax.named_scope("send_inputs"):
+        for to, which in SENDS:
+            pl.when(me != to)(functools.partial(send, to, which))
         for dx, dz in ((0, 1), (0, -1), (1, 0), (-1, 0)):
             tell(near, dx, dz)
-        for to in range(PARTNERS):
-            rows = pl.ds(pl.multiple_of(BAND * spot(to) + ROWS * (2 * core + place), ROWS), ROWS)
-            copy = pltpu.make_async_remote_copy(
-                src_ref=green_stage.at[to % 4],
-                dst_ref=green_all.at[rows],
-                send_sem=green_send,
-                recv_sem=green_recv.at[spot(to) // 2],
-                device_id=partner(to),
-                device_id_type=MESH,
-            )
-            pl.when(me != to)(copy.start)
     field_all[own, :] = field_stage[row]
     green_all[own, :] = green_stage[2 * core + place]
 
@@ -240,7 +240,7 @@
                     phasors[k, at + 128 : at + 160, :] = sin.astype(bf16)
                     return cos * cos1 - sin * sin1, sin * cos1 + cos * sin1
 
-                lax.fori_loop(0, STEPS, step, (slip * cos0, slip * sin0), unroll=8)
+                lax.fori_loop(0, STEPS, step, (slip * cos0, slip * sin0), unroll=32)
 
     with jax.named_scope("along_x"):
         pl.semaphore_wait(line, 2)

time: 28 us -> 27.3 us (0.975)
  Pallas kernels: 26.9 us -> 26.4 us
    pallas_call x1, Pallas kernels: 26.9 us -> 26.4 us  [local(): pl.pallas_call(kernel, out_shape=jax.ShapeDtypeStruct((MOST, 2 * NP), f32...]
where the time goes in v5:
time: 27.3 us; the launch traced here: 27 us
  Pallas kernels  26.4 us (97%)
  local copies, waits for them, and re-layouts  0.6 us (2%)
    pallas_call x1, Pallas kernels, local(): pl.pallas_call(kernel, out_shape=jax.ShapeDtypeStruct((MOST, 2 * NP), f32...  26.4 us
    unnamed x1, local copies, waits for them, and re-layouts  0.6 us

profile of v5, /device:TPU:1, one launch (start us, length us, event | category | flops | bytes accessed | tf_op | source)
XLA Modules:
  0.0 27.0 jit_solution(6903639972160753213)
XLA Ops:
  0.0 26.4 %seismogram.1 = f32[3,512]{1,0:T(4,128)S(1)} custom-call(bf16[16,1024]{1,0:T(8,128)(2,1)} %green_hbm.1, f32[16,256]{1,0:T(8,128)} %slip_hbm.1, f32[16,256]{1,0:T(8,128)} %time_hbm.1, f32[1,256]{1,0:T(1,128)} %bitcast.2, s32[1,256]{1,0:T(1,128)} %bitcast.3), custom_call_target="tpu_custom_call" | custom-call | tf_op jit(solution)/shard_map/seismogram/pallas_call | solution.py:435
  26.4 0.6 %copy.7 = f32[3,512]{1,0:T(4,128)} copy(f32[3,512]{1,0:T(4,128)S(1)} %seismogram.1) | data formatting | bytes 12288

commit v6 on v5

--- a/solution.py
+++ b/solution.py
@@ -147,10 +147,10 @@
         ).start()
 
     with jax.named_scope("send_inputs"):
+        for dx, dz in ((0, 1), (0, -1), (1, 0), (-1, 0)):
+            tell(near, dx, dz)
         for to, which in SENDS:
             pl.when(me != to)(functools.partial(send, to, which))
-        for dx, dz in ((0, 1), (0, -1), (1, 0), (-1, 0)):
-            tell(near, dx, dz)
     field_all[own, :] = field_stage[row]
     green_all[own, :] = green_stage[2 * core + place]
 
@@ -215,6 +215,12 @@
             tell(line, 0, dz)
 
     for band in range(4):
+        if band == 1:
+            with jax.named_scope("along_x"):
+                pl.semaphore_wait(line, 2)
+                for dx in (1, 2, 3):
+                    tell(everyone, dx, 0)
+
         with jax.named_scope("wait_fields"):
             arriving = pl.ds(BAND * band, BAND - ROWS if band == 0 else BAND)
             pltpu.make_async_copy(
@@ -241,11 +247,6 @@
                     return cos * cos1 - sin * sin1, sin * cos1 + cos * sin1
 
                 lax.fori_loop(0, STEPS, step, (slip * cos0, slip * sin0), unroll=32)
-
-    with jax.named_scope("along_x"):
-        pl.semaphore_wait(line, 2)
-        for dx in (1, 2, 3):
-            tell(everyone, dx, 0)
 
     for half in range(2):
         with jax.named_scope("wait_green"):

time: 27.3 us -> 27.1 us (level)
  no operation moved by 1% of the time
where the time goes in v6:
time: 27.1 us; the launch traced here: 26.8 us
  Pallas kernels  26.2 us (97%)
  local copies, waits for them, and re-layouts  0.6 us (2%)
    pallas_call x1, Pallas kernels, local(): pl.pallas_call(kernel, out_shape=jax.ShapeDtypeStruct((MOST, 2 * NP), f32...  26.2 us
    unnamed x1, local copies, waits for them, and re-layouts  0.6 us

profile of v6, /device:TPU:1, one launch (start us, length us, event | category | flops | bytes accessed | tf_op | source)
XLA Modules:
  0.0 26.8 jit_solution(1637278600235558825)
XLA Ops:
  0.0 26.2 %seismogram.1 = f32[3,512]{1,0:T(4,128)S(1)} custom-call(bf16[16,1024]{1,0:T(8,128)(2,1)} %green_hbm.1, f32[16,256]{1,0:T(8,128)} %slip_hbm.1, f32[16,256]{1,0:T(8,128)} %time_hbm.1, f32[1,256]{1,0:T(1,128)} %bitcast.2, s32[1,256]{1,0:T(1,128)} %bitcast.3), custom_call_target="tpu_custom_call" | custom-call | tf_op jit(solution)/shard_map/seismogram/pallas_call | solution.py:436
  26.2 0.6 %copy.7 = f32[3,512]{1,0:T(4,128)} copy(f32[3,512]{1,0:T(4,128)S(1)} %seismogram.1) | data formatting | bytes 12288
